TPU v7x, 32 devices: a whole 2x2x4 slice. The times are simulated.
32 devices in a mesh: group: 2 (over x), blk: 16 (over z, y, core).
Axes of the slice: x: 2, y: 2, z: 4, core: 2. Of those that a mesh axis runs over, the one named last changes fastest.
Arguments:
- traces: bfloat16 [128, 3, 2, 1200], P(('group', 'blk')), may hold values from -180 to 180, as said below
- assign: int32 [128], P(('group', 'blk')), may hold values from 0 to 3, as said below
- matching: int32 [16, 2], P('blk'), may hold values from 0 to 1, as said below
Outputs:
- between: bfloat16 [128, 4, 3, 3, 401], P(('group', 'blk'))
- within: bfloat16 [128, 4, 3, 3, 401], P(('group', 'blk'))
Inputs may be any that keep to these rules, and one draw needn't show every extreme that they name: traces are finite records. `assign`: each aligned block of 4 entries, one device's stations, is a permutation of 0 to 3. `matching`: each row b is one round r_b, 0 to 1, of a round-robin plan with a bye round 0: group g is paired with g XOR r_b.
All inputs are finite; a program needn't handle non-finite values.
Results may differ from a plain program's by a relative error of at most 0.0082.
Values may be sent and summed in bfloat16 or wider, within the bound.
No kernel may reach another device: no remote copies, remote signals or barrier semaphores. Data moves between devices by JAX's collectives and lax.ppermute only.
A program may use at most 64 MiB of HBM per device.

v0:
```python
import math

import jax
import jax.numpy as jnp
from jax import lax
from jax.sharding import PartitionSpec as P

WIN = 2
NSAMP = 1200
PLEN = 1536
NF = 768
HALF = 200
LAGS = 401


EPSILON = 1e-05


def from_behind(block, axis, distance):
    devices = range(lax.axis_size(axis))
    route = [((i - distance) % len(devices), i) for i in devices]
    return lax.ppermute(block, axis, route)


def forward_table():
    sample_ids = jnp.arange(NSAMP, dtype=jnp.int32)[:, None]
    bin_ids = jnp.arange(1, NF + 1, dtype=jnp.int32)[None, :]
    phases = (sample_ids * bin_ids % PLEN).astype(jnp.float32) * (2.0 * math.pi / PLEN)
    return jnp.concatenate([jnp.cos(phases), -jnp.sin(phases)], axis=1).astype(jnp.bfloat16)


def inverse_table():
    bin_ids = jnp.arange(1, NF + 1, dtype=jnp.int32)[:, None]
    lag_ids = jnp.arange(LAGS, dtype=jnp.int32)[None, :] - HALF
    phases = (bin_ids * lag_ids % PLEN).astype(jnp.float32) * (2.0 * math.pi / PLEN)
    return jnp.concatenate([jnp.cos(phases), -jnp.sin(phases)], axis=0).astype(jnp.bfloat16)


def transform(normal, forward):
    flat_rows = normal.reshape(-1, normal.shape[-1])
    result = jnp.dot(flat_rows, forward, preferred_element_type=jnp.float32).astype(jnp.bfloat16)
    return result.reshape(normal.shape[:-1] + (forward.shape[1],))


def correlate(local_spec, remote_spec, inverse):
    half_bins = local_spec.shape[-1] // 2
    left = local_spec.astype(jnp.float32)[:, None, :, None, :, :]
    right = remote_spec.astype(jnp.float32)[None, :, None, :, :, :]
    left_re, left_im = (left[..., :half_bins], left[..., half_bins:])
    right_re, right_im = (right[..., :half_bins], right[..., half_bins:])
    real_part = jnp.sum(left_re * right_re + left_im * right_im, axis=4)
    imag_part = jnp.sum(left_re * right_im - left_im * right_re, axis=4)
    stacked = jnp.concatenate([real_part, imag_part], axis=-1).astype(jnp.bfloat16)
    lag_scale = 2.0 / (PLEN * math.sqrt(NSAMP * WIN))
    lag_values = (
        jnp.dot(stacked.reshape(-1, 2 * half_bins), inverse, preferred_element_type=jnp.float32)
        * lag_scale
    )
    return lag_values.astype(jnp.bfloat16).reshape(
        local_spec.shape[0], remote_spec.shape[0], 3, 3, inverse.shape[1]
    )


def shards(traces, assign, matching):
    station_count = traces.shape[0]
    forward = forward_table()
    inverse = inverse_table()
    slot_ids = jnp.arange(station_count, dtype=jnp.int32)
    onehot = (assign[None, :] == slot_ids[:, None]).astype(jnp.bfloat16)
    ordered = jnp.einsum("sr,rcwt->scwt", onehot, traces, preferred_element_type=jnp.float32)
    energy = jnp.mean(ordered * ordered, axis=-1, keepdims=True)
    normal = (ordered * lax.rsqrt(energy + EPSILON)).astype(jnp.bfloat16)
    spectra = transform(normal, forward)
    group_index = lax.axis_index("group")
    partner_row = matching[0]
    everything = lax.all_gather(spectra, "group", axis=0, tiled=True)
    offset = partner_row[group_index] * station_count
    remote = lax.dynamic_slice_in_dim(everything, offset, station_count, 0)
    beside = from_behind(spectra, "blk", 1)
    between = correlate(spectra, remote, inverse)
    within = correlate(spectra, beside, inverse)
    return (between, within)


def solution(mesh):
    placed = (P(("group", "blk"), None, None, None), P(("group", "blk")), P("blk", None))
    return jax.shard_map(
        shards,
        mesh=mesh,
        in_specs=placed,
        out_specs=(
            P(("group", "blk"), None, None, None, None),
            P(("group", "blk"), None, None, None, None),
        ),
        check_vma=False,
    )
```

profile of v0, /device:TPU:1, one launch (start us, length us, event | category | flops | bytes accessed | tf_op | source)
XLA Modules:
  0.0 41.9 jit_solution(13991110612467681651)
XLA Ops:
  0.6 0.0 copy-start
  0.7 0.0 copy-start.1
  0.7 16.3 %cosine_convert_fusion = (bf16[1200,768]{1,0:T(8,128)(2,1)S(1)}, bf16[1200,768]{1,0:T(8,128)(2,1)}) fusion(s32[768]{0:T(1024)S(1)} %iota_add_fusion), kind=kLoop, calls=%fused_computation.8 | loop fusion | flops 11059200 | bytes 3689472 | tf_op jit(solution)/shard_map/convert.13
  16.9 0.0 copy-done
  17.0 0.0 copy-done.1
  17.0 0.2 multiply_reduce_fusion
  17.2 0.1 multiply_convert_fusion
  17.4 0.0 copy-start.2
  17.4 2.1 %fusion.9 = bf16[24,1536]{1,0:T(8,128)(2,1)S(1)} fusion(bf16[24,1200]{1,0:T(8,128)(2,1)S(1)} %reshape.64, bf16[1200,768]{1,0:T(8,128)(2,1)} %get-tuple-element.25, bf16[1200,768]{1,0:T(8,128)(2,1)S(1)} %get-tuple-element.24), kind=kOutput, calls=%fused_computation.14 | convolution fusion | flops 95883264 | bytes 3817728 | tf_op jit(solution)/shard_map/dot_general | solution.py:41
  19.6 2.7 %collective-permute-start = (bf16[4,3,2,1536]{3,2,1,0:T(2,128)(2,1)S(1)}, bf16[4,3,2,1536]{3,2,1,0:T(2,128)(2,1)S(1)}, u32[]{:S(2)}, u32[]{:S(2)}) collective-permute-start(bf16[4,3,2,1536]{3,2,1,0:T(2,128)(2,1)S(1)} %reshape.65), channel_id=1, source_target_pairs={{15,0},{0,1},{1,2},{2,3},{3,4},{4,5},{5,6},{6,7},{7,8},{8,9},{9,10... | collective-permute-start | bytes 221192 | tf_op jit(solution)/shard_map/ppermute | solution.py:22
  22.3 4.2 %all_gather.3 = bf16[8,3,2,1536]{3,2,1,0:T(2,128)(2,1)S(1)} all-gather(bf16[4,3,2,1536]{3,2,1,0:T(2,128)(2,1)S(1)} %reshape.65), channel_id=1, replica_groups=mesh['group'=2,'blk'=16] {'group'}, dimensions={0}, use_global_device_ids=true | all-gather | bytes 221184 | tf_op jit(solution)/shard_map/all_gather | solution.py:76
  26.4 0.1 reshape.68
  26.5 0.0 copy-done.2
  26.6 0.6 %fusion.33 = s32[1,1]{1,0:T(1,128)} fusion(s32[1,2]{1,0:T(1,128)S(1)} %copy-done.2, s32[]{:T(128)S(6)} %select_n.24), kind=kLoop, calls=%fused_computation.60 | loop fusion | flops 1 | bytes 12 | tf_op jit(solution)/shard_map/mul | solution.py:77
  29.1 0.1 bitcast_convert_fusion.1
  29.2 7.1 %cosine_convert_fusion.1 = (bf16[768,401]{1,0:T(8,128)(2,1)S(1)}, bf16[768,401]{1,0:T(8,128)(2,1)S(1)}) fusion(s32[401]{0:T(512)S(1)} %iota_add_fusion.1, s32[768]{0:T(1024)S(1)} %iota_add_fusion), kind=kLoop, calls=%fused_computation.19 | loop fusion | flops 3695616 | bytes 1236548 | tf_op jit(solution)/shard_map/convert.7
  36.3 0.0 collective-permute-done
  36.3 0.1 bitcast_convert_fusion
  36.5 1.7 %add_reduce_fusion = (bf16[4,4,3,3,768]{4,1,3,2,0:T(4,128)(2,1)S(1)}, bf16[4,4,3,3,768]{4,1,3,2,0:T(4,128)(2,1)S(1)}, bf16[4,4,3,3,768]{4,1,3,2,0:T(4,128)(2,1)S(1)}, bf16[4,4,3,3,768]{4,1,3,2,0:T(4,128)(2,1)S(1)}) fusion(f32[4,3,2,768]{3,0,2,1:T(4,128)S(1)} %copy.23, f32[4,3,2,768]{3,0,2,1:T(4,128)S(1)} %copy.22, ...), kind=kLoop, calls=%fused_computation.29 | loop fusion | flops 3096576 | bytes 1327104 | tf_op jit(solution)/shard_map/reduce_sum | solution.py:51
  38.1 0.1 copy.24
  38.3 0.2 concatenate.31
  38.5 0.1 copy.25
  38.6 0.2 concatenate.32
  38.8 0.4 fusion.18
  39.2 0.1 reshape.67
  39.3 0.7 %copy.27 = bf16[4,4,3,3,401]{4,1,3,2,0:T(4,128)(2,1)} copy(bf16[4,4,3,3,401]{4,3,2,1,0:T(4,128)(2,1)S(1)} %reshape.67) | data formatting | bytes 230976
  40.0 0.1 copy.20
  40.1 0.2 concatenate.27
  40.3 0.1 copy.21
  40.4 0.2 concatenate.28
  40.6 0.4 fusion.17
  41.1 0.1 reshape.66
  41.1 0.7 %copy.26 = bf16[4,4,3,3,401]{4,1,3,2,0:T(4,128)(2,1)} copy(bf16[4,4,3,3,401]{4,3,2,1,0:T(4,128)(2,1)S(1)} %reshape.66) | data formatting | bytes 230976
  (13 shorter events, 0.3 us)
Async XLA Ops:
  0.6 16.3 %copy-start = (bf16[4,3,2,1200]{3,2,1,0:T(2,128)(2,1)S(1)}, bf16[4,3,2,1200]{3,2,1,0:T(2,128)(2,1)}, u32[]{:S(2)}) copy-start(bf16[4,3,2,1200]{3,2,1,0:T(2,128)(2,1)} %param.3) | copy-start | bytes 172804
  0.7 16.3 %copy-start.1 = (s32[4]{0:T(128)S(1)}, s32[4]{0:T(128)}, u32[]{:S(2)}) copy-start(s32[4]{0:T(128)} %param.4) | copy-start | bytes 52
  17.4 9.1 %copy-start.2 = (s32[1,2]{1,0:T(1,128)S(1)}, s32[1,2]{1,0:T(1,128)}, u32[]{:S(2)}) copy-start(s32[1,2]{1,0:T(1,128)} %param.5) | copy-start | bytes 28
  19.6 16.8 %collective-permute-start = (bf16[4,3,2,1536]{3,2,1,0:T(2,128)(2,1)S(1)}, bf16[4,3,2,1536]{3,2,1,0:T(2,128)(2,1)S(1)}, u32[]{:S(2)}, u32[]{:S(2)}) collective-permute-start(bf16[4,3,2,1536]{3,2,1,0:T(2,128)(2,1)S(1)} %reshape.65), channel_id=1, source_target_pairs={{15,0},{0,1},{1,2},{2,3},{3,4},{4,5},{5,6},{6,7},{7,8},{8,9},{9,10... | collective-permute-start | bytes 221192 | tf_op jit(solution)/shard_map/ppermute | solution.py:22
where the time goes:
time: 42.1 us; the launch traced here: 41.9 us
  other arithmetic  25.8 us (61%)
  blocking collectives  4.16 us (10%)
  local copies, waits for them, and re-layouts  3.24 us (8%)
  matrix products  3.16 us (8%)
  between operations  2.81 us (7%)
  starting transfers between devices  2.68 us (6%)
    another operation x2, other arithmetic  23.3 us
    all_gather x1, blocking collectives, shards(): everything = lax.all_gather(spectra, 'group', axis=0, tiled=True)  4.16 us
    ppermute x1, starting transfers between devices, from_behind(): return lax.ppermute(block, axis, route)  2.68 us
    dot_general x1, matrix products, transform(): jnp.dot(flat_rows, forward, preferred_element_type=jnp.float32)  2.1 us
    reduce_sum x1, other arithmetic, correlate(): real_part = jnp.sum(left_re * right_re + left_im * right_im, axis=4)  1.65 us
    unnamed x8, local copies, waits for them, and re-layouts  1.47 us
  transfers between devices with their start and end apart: 1, of which 0 were waited for; matrix products, arithmetic and copies ran while one was open for 19% of the time, Pallas kernels for 0%

commit v1 on v0

v1 whole, which is shorter than its diff:
```python
import functools
import math

import jax
import jax.numpy as jnp
import ml_dtypes
import numpy as np
from jax import lax
from jax.experimental import pallas as pl
from jax.experimental.pallas import tpu as pltpu
from jax.sharding import PartitionSpec as P

STA = 4
COMP = 3
WIN = 2
NSAMP = 1200
PLEN = 1536
NF = 768
HALF = 200
LAGS = 401
ROWS = 16

EPSILON = 1e-05
LAG_SCALE = 2.0 / (PLEN * math.sqrt(NSAMP * WIN))


def forward_table():
    phases = np.arange(NSAMP)[:, None] * np.arange(1, NF + 1)[None, :] % PLEN * (2.0 * math.pi / PLEN)
    return np.concatenate([np.cos(phases), -np.sin(phases)], axis=1).astype(ml_dtypes.bfloat16)


def inverse_table():
    lags = np.arange(LAGS) - HALF
    phases = np.arange(1, NF + 1)[:, None] * lags[None, :] % PLEN * (2.0 * math.pi / PLEN)
    return np.concatenate([np.cos(phases), -np.sin(phases)], axis=0).astype(ml_dtypes.bfloat16)


def spectra_of(rows, forward):
    values = rows.astype(jnp.float32)
    energy = jnp.sum(values * values, axis=-1, keepdims=True) * (1.0 / NSAMP)
    normal = (values * lax.rsqrt(energy + EPSILON)).astype(jnp.bfloat16)
    result = jnp.dot(normal, forward, preferred_element_type=jnp.float32)
    return result.astype(jnp.bfloat16).astype(jnp.float32)


def own_kernel(rows_ref, forward_ref, spectra_ref):
    spectra_ref[...] = spectra_of(rows_ref[...], forward_ref[...])


def pair_kernel(rows_ref, left_ref, forward_ref, inverse_ref, out_ref, cross_ref):
    right = spectra_of(rows_ref[...], forward_ref[...])
    right_re = [right[w * ROWS : (w + 1) * ROWS, :NF] for w in range(WIN)]
    right_im = [right[w * ROWS : (w + 1) * ROWS, NF:] for w in range(WIN)]
    for a in range(STA):
        for i in range(COMP):
            real = jnp.zeros((ROWS, NF), jnp.float32)
            imag = jnp.zeros((ROWS, NF), jnp.float32)
            for w in range(WIN):
                row = w * ROWS + i * STA + a
                left_re = left_ref[row : row + 1, :NF]
                left_im = left_ref[row : row + 1, NF:]
                real += left_re * right_re[w] + left_im * right_im[w]
                imag += left_re * right_im[w] - left_im * right_re[w]
            base = (a * COMP + i) * ROWS
            cross_ref[base : base + ROWS, :NF] = real.astype(jnp.bfloat16)
            cross_ref[base : base + ROWS, NF:] = imag.astype(jnp.bfloat16)
    lags = jnp.dot(cross_ref[...], inverse_ref[...], preferred_element_type=jnp.float32) * LAG_SCALE
    for a in range(STA):
        for i in range(COMP):
            for j in range(COMP):
                row = (a * COMP + i) * ROWS + j * STA
                out_ref[a, i, j] = lags[row : row + STA].astype(jnp.bfloat16)


def in_vmem():
    return pl.BlockSpec(memory_space=pltpu.VMEM)


def own_spectra(rows, forward):
    return pl.pallas_call(
        own_kernel,
        out_shape=jax.ShapeDtypeStruct((WIN * ROWS, 2 * NF), jnp.float32),
        in_specs=[in_vmem()] * 2,
        out_specs=in_vmem(),
        compiler_params=pltpu.CompilerParams(vmem_limit_bytes=24 * 2**20),
        cost_estimate=pl.CostEstimate(flops=2 * 32 * NSAMP * 2 * NF, bytes_accessed=4_000_000, transcendentals=0),
    )(rows, forward)


def correlate(rows, left, forward, inverse):
    out = pl.pallas_call(
        pair_kernel,
        out_shape=jax.ShapeDtypeStruct((STA, COMP, COMP, STA, LAGS), jnp.bfloat16),
        in_specs=[in_vmem()] * 4,
        out_specs=in_vmem(),
        scratch_shapes=[pltpu.VMEM((STA * COMP * ROWS, 2 * NF), jnp.bfloat16)],
        compiler_params=pltpu.CompilerParams(vmem_limit_bytes=24 * 2**20),
        cost_estimate=pl.CostEstimate(flops=600_000_000, bytes_accessed=6_000_000, transcendentals=0),
    )(rows, left, forward, inverse)
    return out.transpose(0, 3, 1, 2, 4)


def shards(groups, blocks, traces, assign, matching):
    forward = jnp.asarray(forward_table())
    inverse = jnp.asarray(inverse_table())
    onehot = (assign[None, :] == jnp.arange(STA, dtype=jnp.int32)[:, None]).astype(jnp.bfloat16)
    ordered = jnp.einsum("sr,rcwt->wcst", onehot, traces, preferred_element_type=jnp.float32).astype(jnp.bfloat16)
    rows = jnp.pad(ordered.reshape(WIN, COMP * STA, NSAMP), ((0, 0), (0, ROWS - COMP * STA), (0, 0)))
    rows = rows.reshape(WIN * ROWS, NSAMP)
    beside = lax.ppermute(rows, "blk", [((i - 1) % blocks, i) for i in range(blocks)])
    remote = rows
    step = 1
    while step < groups:
        other = lax.ppermute(remote, "group", [(g ^ step, g) for g in range(groups)])
        remote = jnp.where((matching[0, 0] & step) != 0, other, remote)
        step *= 2
    left = own_spectra(rows, forward)
    between = correlate(remote, left, forward, inverse)
    within = correlate(beside, left, forward, inverse)
    return (between, within)


def solution(mesh):
    placed = (P(("group", "blk"), None, None, None), P(("group", "blk")), P("blk", None))
    return jax.shard_map(
        functools.partial(shards, mesh.shape["group"], mesh.shape["blk"]),
        mesh=mesh,
        in_specs=placed,
        out_specs=(
            P(("group", "blk"), None, None, None, None),
            P(("group", "blk"), None, None, None, None),
        ),
        check_vma=False,
    )
```

time: 42.1 us -> 17 us (0.40)
  other arithmetic: 25.8 us -> 0.02 us
  Pallas kernels: 0 us -> 4.76 us
  blocking collectives: 4.16 us -> 0 us
  matrix products: 3.16 us -> 0.81 us
  local copies, waits for them, and re-layouts: 3.24 us -> 5.53 us
  starting transfers between devices: 2.68 us -> 4.19 us
  between operations: 2.81 us -> 1.36 us
    another operation x2 -> x0, other arithmetic: 23.3 us -> none
    pallas_call x0 -> x3, Pallas kernels: none -> 4.76 us  [the longest x2 3.94 us: correlate(): pl.pallas_call(pair_kernel, out_shape=jax.ShapeDtypeStruct((STA, COMP, CO...]
    all_gather x1 -> x0, blocking collectives: 4.16 us -> none  [shards(): everything = lax.all_gather(spectra, 'group', axis=0, tiled=True)]
    unnamed x8 -> x11, local copies, waits for them, and re-layouts: 1.47 us -> 5.47 us
    dot_general x4 -> x1, matrix products: 3.16 us -> 0.81 us  [shards(): jnp.einsum('sr,rcwt->wcst', onehot, traces, preferred_element_type=jnp.fl...]
    reduce_sum x1 -> x0, other arithmetic: 1.65 us -> none  [correlate(): real_part = jnp.sum(left_re * right_re + left_im * right_im, axis=4)]
    ppermute x1 -> x2, starting transfers between devices: 2.68 us -> 4.19 us  [the longest x1 2.11 us: shards(): lax.ppermute(remote, 'group', [(g ^ step, g) for g in range(groups)])]
    concatenate x4 -> x0, local copies, waits for them, and re-layouts: 0.75 us -> none  [correlate(): jnp.concatenate([real_part, imag_part], axis=-1).astype(jnp.bfloat16)]
  transfers between devices with their start and end apart: 1 -> 2, of which waited for: 0 -> 0; matrix products, arithmetic and copies ran while one was open for 19% -> 0% of each run, Pallas kernels for 0% -> 17%
where the time goes in v1:
time: 17 us; the launch traced here: 16.7 us
  local copies, waits for them, and re-layouts  5.53 us (33%)
  Pallas kernels  4.76 us (28%)
  starting transfers between devices  4.19 us (25%)
  between operations  1.36 us (8%)
  matrix products  0.81 us (5%)
    unnamed x11, local copies, waits for them, and re-layouts  5.47 us
    pallas_call x2, Pallas kernels, correlate(): pl.pallas_call(pair_kernel, out_shape=jax.ShapeDtypeStruct((STA, COMP, CO...  3.94 us
    ppermute x1, starting transfers between devices, shards(): lax.ppermute(remote, 'group', [(g ^ step, g) for g in range(groups)])  2.11 us
    ppermute x1, starting transfers between devices, shards(): lax.ppermute(rows, 'blk', [((i - 1) % blocks, i) for i in range(blocks)])  2.08 us
    pallas_call x1, Pallas kernels, own_spectra(): pl.pallas_call(own_kernel, out_shape=jax.ShapeDtypeStruct((WIN * ROWS, 2...  0.82 us
    dot_general x1, matrix products, shards(): jnp.einsum('sr,rcwt->wcst', onehot, traces, preferred_element_type=jnp.fl...  0.81 us
  transfers between devices with their start and end apart: 2, of which 0 were waited for; matrix products, arithmetic and copies ran while one was open for 0% of the time, Pallas kernels for 17%

profile of v1, /device:TPU:1, one launch (start us, length us, event | category | flops | bytes accessed | tf_op | source)
XLA Modules:
  0.0 16.7 jit_solution(6942023113711112580)
XLA Ops:
  0.6 0.0 copy-start
  0.6 0.8 %copy-done = bf16[4,3,2,1200]{3,2,1,0:T(2,128)(2,1)S(1)} copy-done((bf16[4,3,2,1200]{3,2,1,0:T(2,128)(2,1)S(1)}, bf16[4,3,2,1200]{3,2,1,0:T(2,128)(2,1)}, u32[]{:S(2)}) %copy-start) | copy-done | bytes 57624
  1.5 0.8 %fusion = bf16[2,3,4,1200]{3,2,0,1:T(4,128)(2,1)S(1)} fusion(bf16[4,3,2,1200]{3,2,1,0:T(2,128)(2,1)S(1)} %copy-done, s32[4]{0:T(128)} %param.6), kind=kOutput, calls=%fused_computation.1 | convolution fusion | flops 259216 | bytes 115216 | tf_op jit(solution)/shard_map/sr,rcwt->wcst/dot_general | solution.py:107
  2.4 2.1 %collective-permute-start = (bf16[32,1200]{1,0:T(8,128)(2,1)S(1)}, bf16[32,1200]{1,0:T(8,128)(2,1)S(1)}, u32[]{:S(2)}, u32[]{:S(2)}) collective-permute-start(bf16[32,1200]{1,0:T(8,128)(2,1)S(1)} %bitcast.14), channel_id=1, source_target_pairs={{16,0},{0,16},{17,1},{1,17},{18,2},{2,18},{19,3},{3,19},{20,4},{4,... | collective-permute-start | bytes 230408 | tf_op jit(solution)/shard_map/ppermute | solution.py:114
  4.5 2.1 %collective-permute-start.1 = (bf16[32,1200]{1,0:T(8,128)(2,1)S(1)}, bf16[32,1200]{1,0:T(8,128)(2,1)S(1)}, u32[]{:S(2)}, u32[]{:S(2)}) collective-permute-start(bf16[32,1200]{1,0:T(8,128)(2,1)S(1)} %bitcast.15), channel_id=1, source_target_pairs={{15,0},{0,1},{1,2},{2,3},{3,4},{4,5},{5,6},{6,7},{7,8},{8,9},{9,10... | collective-permute-start | bytes 230408 | tf_op jit(solution)/shard_map/ppermute | solution.py:110
  7.2 0.0 copy-start.1
  7.2 2.0 %copy-done.1 = bf16[1200,1536]{1,0:T(8,128)(2,1)S(1)} copy-done((bf16[1200,1536]{1,0:T(8,128)(2,1)S(1)}, bf16[1200,1536]{1,0:T(8,128)(2,1)}, u32[]{:S(2)}) %copy-start.1) | copy-done | bytes 3686424
  9.3 0.0 copy-start.2
  9.3 0.8 %shard_map.68.left_ref = f32[32,1536]{1,0:T(8,128)S(1)} custom-call(bf16[32,1200]{1,0:T(8,128)(2,1)S(1)} %bitcast.16, bf16[1200,1536]{1,0:T(8,128)(2,1)S(1)} %copy-done.1), custom_call_target="tpu_custom_call" | custom-call | flops 117964800 | bytes 4000000 | tf_op jit(solution)/shard_map/pallas_call | solution.py:80
  10.1 0.0 collective-permute-done
  10.1 1.2 %copy-done.2 = bf16[1200,1536]{1,0:T(8,128)(2,1)S(1)} copy-done((bf16[1200,1536]{1,0:T(8,128)(2,1)S(1)}, bf16[1200,1536]{1,0:T(8,128)(2,1)}, u32[]{:S(2)}) %copy-start.2) | copy-done | bytes 3686424
  11.3 0.0 copy-start.3
  11.3 1.4 %copy-done.3 = bf16[1536,401]{1,0:T(8,128)(2,1)S(1)} copy-done((bf16[1536,401]{1,0:T(8,128)(2,1)S(1)}, bf16[1536,401]{1,0:T(8,128)(2,1)}, u32[]{:S(2)}) %copy-start.3) | copy-done | bytes 1231896
  12.7 0.0 copy-start.4
  12.7 2.0 %shard_map.69 = bf16[4,3,3,4,401]{4,3,2,1,0:T(4,128)(2,1)} custom-call(bf16[32,1200]{1,0:T(8,128)(2,1)S(1)} %broadcast_select_fusion.rows_ref, f32[32,1536]{1,0:T(8,128)S(1)} %shard_map.68.left_ref, bf16[1200,1536]{1,0:T(8,128)(2,1)S(1)} %copy-done.2, bf16[1536,401]{1,0:T(8,128)(2,1)S(1)} %copy-done.3), custom_call_target="tpu_custom_call" | custom-call | flops 600000000 | bytes 6000000 | tf_op jit(solution)/shard_map/pallas_call | solution.py:91
  14.7 0.0 collective-permute-done.1.rows_ref
  14.7 0.0 copy-done.4
  14.7 2.0 %shard_map.70 = bf16[4,3,3,4,401]{4,3,2,1,0:T(4,128)(2,1)} custom-call(bf16[32,1200]{1,0:T(8,128)(2,1)S(1)} %collective-permute-done.1.rows_ref, f32[32,1536]{1,0:T(8,128)S(1)} %shard_map.68.left_ref, bf16[1200,1536]{1,0:T(8,128)(2,1)S(1)} %copy-done.2, bf16[1536,401]{1,0:T(8,128)(2,1)S(1)} %copy-done.4), custom_call_target="tpu_custom_call" | custom-call | flops 600000000 | bytes 6000000 | tf_op jit(solution)/shard_map/pallas_call | solution.py:91
  (4 shorter events, 0.1 us)
Async XLA Ops:
  0.6 0.8 %copy-start = (bf16[4,3,2,1200]{3,2,1,0:T(2,128)(2,1)S(1)}, bf16[4,3,2,1200]{3,2,1,0:T(2,128)(2,1)}, u32[]{:S(2)}) copy-start(bf16[4,3,2,1200]{3,2,1,0:T(2,128)(2,1)} %param.5) | copy-start | bytes 172804
  2.4 7.7 %collective-permute-start = (bf16[32,1200]{1,0:T(8,128)(2,1)S(1)}, bf16[32,1200]{1,0:T(8,128)(2,1)S(1)}, u32[]{:S(2)}, u32[]{:S(2)}) collective-permute-start(bf16[32,1200]{1,0:T(8,128)(2,1)S(1)} %bitcast.14), channel_id=1, source_target_pairs={{16,0},{0,16},{17,1},{1,17},{18,2},{2,18},{19,3},{3,19},{20,4},{4,... | collective-permute-start | bytes 230408 | tf_op jit(solution)/shard_map/ppermute | solution.py:114
  4.5 10.2 %collective-permute-start.1 = (bf16[32,1200]{1,0:T(8,128)(2,1)S(1)}, bf16[32,1200]{1,0:T(8,128)(2,1)S(1)}, u32[]{:S(2)}, u32[]{:S(2)}) collective-permute-start(bf16[32,1200]{1,0:T(8,128)(2,1)S(1)} %bitcast.15), channel_id=1, source_target_pairs={{15,0},{0,1},{1,2},{2,3},{3,4},{4,5},{5,6},{6,7},{7,8},{8,9},{9,10... | collective-permute-start | bytes 230408 | tf_op jit(solution)/shard_map/ppermute | solution.py:110
  7.2 2.0 %copy-start.1 = (bf16[1200,1536]{1,0:T(8,128)(2,1)S(1)}, bf16[1200,1536]{1,0:T(8,128)(2,1)}, u32[]{:S(2)}) copy-start(bf16[1200,1536]{1,0:T(8,128)(2,1)} %constant.12.clone.forward_ref) | copy-start | bytes 11059204
  9.3 2.0 %copy-start.2 = (bf16[1200,1536]{1,0:T(8,128)(2,1)S(1)}, bf16[1200,1536]{1,0:T(8,128)(2,1)}, u32[]{:S(2)}) copy-start(bf16[1200,1536]{1,0:T(8,128)(2,1)} %constant.12.clone.forward_ref) | copy-start | bytes 11059204
  11.3 1.4 %copy-start.3 = (bf16[1536,401]{1,0:T(8,128)(2,1)S(1)}, bf16[1536,401]{1,0:T(8,128)(2,1)}, u32[]{:S(2)}) copy-start(bf16[1536,401]{1,0:T(8,128)(2,1)} %constant.13.clone.inverse_ref) | copy-start | bytes 3695620
  12.7 2.0 %copy-start.4 = (bf16[1536,401]{1,0:T(8,128)(2,1)S(1)}, bf16[1536,401]{1,0:T(8,128)(2,1)}, u32[]{:S(2)}) copy-start(bf16[1536,401]{1,0:T(8,128)(2,1)} %constant.13.clone.inverse_ref) | copy-start | bytes 3695620

commit v2 on v1

v2 whole, which is shorter than its diff:
```python
import functools
import math

import jax
import jax.numpy as jnp
import ml_dtypes
import numpy as np
from jax import lax
from jax.experimental import pallas as pl
from jax.experimental.pallas import tpu as pltpu
from jax.sharding import PartitionSpec as P

STA = 4
COMP = 3
WIN = 2
NSAMP = 1200
PLEN = 1536
FOLD = PLEN // 2
NF = 768
QUARTER = NF // 2
HALF = 200
LAGS = 401
STEP = COMP * STA
LONG = 1280

EPSILON = 1e-05
LAG_SCALE = 2.0 / (PLEN * math.sqrt(NSAMP * WIN))

EVEN_BINS = np.arange(2, NF + 1, 2)
ODD_BINS = np.arange(1, NF + 1, 2)


def turned(ids_a, ids_b):
    phases = ids_a[:, None] * ids_b[None, :] % PLEN * (2.0 * math.pi / PLEN)
    return np.cos(phases), np.sin(phases)


def forward_table(bins):
    cosine, sine = turned(np.arange(FOLD), bins)
    return np.concatenate([cosine, -sine], axis=1).astype(ml_dtypes.bfloat16)


def inverse_table():
    lags = np.arange(LAGS) - HALF
    parts = []
    for bins in (EVEN_BINS, ODD_BINS):
        cosine, sine = turned(bins, lags)
        parts += [cosine, -sine]
    return np.concatenate(parts, axis=0).astype(ml_dtypes.bfloat16)


def spectra_of(rows, even_ref, odd_ref):
    values = rows.astype(jnp.float32)
    energy = jnp.sum(values * values, axis=-1, keepdims=True) * (1.0 / NSAMP)
    normal = values * lax.rsqrt(energy + EPSILON)
    early = normal[:, :FOLD]
    late = jnp.concatenate(
        [normal[:, FOLD:], jnp.zeros((rows.shape[0], PLEN - rows.shape[1]), jnp.float32)], axis=1
    )
    total = (early + late).astype(jnp.bfloat16)
    change = (early - late).astype(jnp.bfloat16)
    even = jnp.dot(total, even_ref[...], preferred_element_type=jnp.float32)
    odd = jnp.dot(change, odd_ref[...], preferred_element_type=jnp.float32)
    result = jnp.concatenate([even, odd], axis=1)
    return result.astype(jnp.bfloat16).astype(jnp.float32)


def cross_and_back(right, left_ref, inverse_ref, out_ref, cross_ref):
    first = lax.broadcasted_iota(jnp.int32, (2 * STEP, QUARTER), 0) < STEP
    for h in range(2):
        parts = []
        for begin in (h * NF, h * NF + QUARTER):
            for w in range(WIN):
                part = right[w * STEP : (w + 1) * STEP, begin : begin + QUARTER]
                parts.append(jnp.concatenate([part, part], axis=0))
        right_re, right_im = parts[:WIN], parts[WIN:]
        re, im = h * NF, h * NF + QUARTER
        for pair in range(STEP // 2):
            real = imag = None
            for w in range(WIN):
                rows = []
                for q in (2 * pair, 2 * pair + 1):
                    rows.append(w * STEP + q % COMP * STA + q // COMP)
                left_re = jnp.where(first, left_ref[rows[0] : rows[0] + 1, re : re + QUARTER], left_ref[rows[1] : rows[1] + 1, re : re + QUARTER])
                left_im = jnp.where(first, left_ref[rows[0] : rows[0] + 1, im : im + QUARTER], left_ref[rows[1] : rows[1] + 1, im : im + QUARTER])
                more_real = left_re * right_re[w] + left_im * right_im[w]
                more_imag = left_re * right_im[w] - left_im * right_re[w]
                real = more_real if real is None else real + more_real
                imag = more_imag if imag is None else imag + more_imag
            base = pair * 2 * STEP
            cross_ref[base : base + 2 * STEP, re : re + QUARTER] = real.astype(jnp.bfloat16)
            cross_ref[base : base + 2 * STEP, im : im + QUARTER] = imag.astype(jnp.bfloat16)
    lags = jnp.dot(cross_ref[...], inverse_ref[...], preferred_element_type=jnp.float32) * LAG_SCALE
    for a in range(STA):
        for i in range(COMP):
            for j in range(COMP):
                row = (a * COMP + i) * STEP + j * STA
                out_ref[a, i, j] = lags[row : row + STA].astype(jnp.bfloat16)


def order_kernel(traces_ref, assign_ref, long_ref, rows_ref, held, order, sems):
    fetch = pltpu.make_async_copy(traces_ref, held, sems.at[0])
    fetch_order = pltpu.make_async_copy(assign_ref, order, sems.at[1])
    fetch.start()
    fetch_order.start()
    fetch_order.wait()
    count = WIN * STEP
    row = lax.broadcasted_iota(jnp.int32, (count, count), 0)
    col = lax.broadcasted_iota(jnp.int32, (count, count), 1)
    target = col % WIN * STEP + col // WIN % COMP * STA
    for r in range(STA):
        target += jnp.where(col // (COMP * WIN) == r, order[0:1, r : r + 1], 0)
    move = (row == target).astype(jnp.float32).astype(jnp.bfloat16)
    fetch.wait()
    records = held[...].astype(jnp.float32).reshape(count, NSAMP).astype(jnp.bfloat16)
    placed = jnp.dot(move, records, preferred_element_type=jnp.float32).astype(jnp.bfloat16)
    rows_ref[...] = placed
    long_ref[...] = jnp.concatenate([placed, jnp.zeros((count, long_ref.shape[1] - NSAMP), jnp.bfloat16)], axis=1)


def own_kernel(rows_ref, even_ref, odd_ref, left_ref):
    left_ref[...] = spectra_of(rows_ref[...], even_ref, odd_ref)


def between_kernel(bit, rows_ref, left_ref, matching_ref, even_ref, odd_ref, inverse_ref, out_ref, cross_ref):
    other = spectra_of(rows_ref[...], even_ref, odd_ref)
    away = (matching_ref[:, 0:1] & bit) != 0
    right = jnp.where(away, other, left_ref[...])
    cross_and_back(right, left_ref, inverse_ref, out_ref, cross_ref)


def within_kernel(rows_ref, left_ref, even_ref, odd_ref, inverse_ref, between_ref, out_ref, between_out_ref, cross_ref, sem):
    leave = pltpu.make_async_copy(between_ref, between_out_ref, sem)
    leave.start()
    right = spectra_of(rows_ref[...], even_ref, odd_ref)
    cross_and_back(right, left_ref, inverse_ref, out_ref, cross_ref)
    leave.wait()


def in_vmem():
    return pl.BlockSpec(memory_space=pltpu.VMEM)


def in_hbm():
    return pl.BlockSpec(memory_space=pltpu.HBM)


OUT = jax.ShapeDtypeStruct((STA, COMP, COMP, STA, LAGS), jnp.bfloat16)
CROSS = pltpu.VMEM((STA * COMP * STEP, 2 * NF), jnp.bfloat16)


def params():
    return pltpu.CompilerParams(vmem_limit_bytes=24 * 2**20)


def order_rows(traces, assign):
    return pl.pallas_call(
        order_kernel,
        out_shape=[
            jax.ShapeDtypeStruct((WIN * STEP, LONG), jnp.bfloat16),
            jax.ShapeDtypeStruct((WIN * STEP, NSAMP), jnp.bfloat16),
        ],
        in_specs=[in_hbm(), in_hbm()],
        out_specs=[in_vmem(), in_vmem()],
        scratch_shapes=[
            pltpu.VMEM((STA, COMP, WIN, NSAMP), jnp.bfloat16),
            pltpu.VMEM((1, STA), jnp.int32),
            pltpu.SemaphoreType.DMA((2,)),
        ],
        compiler_params=params(),
        cost_estimate=pl.CostEstimate(flops=8_000_000_000, bytes_accessed=20_000_000, transcendentals=0),
    )(
        pltpu.with_memory_space_constraint(traces, pltpu.HBM),
        pltpu.with_memory_space_constraint(assign.reshape(1, STA), pltpu.HBM),
    )


def own_spectra(rows, even, odd):
    return pl.pallas_call(
        own_kernel,
        out_shape=jax.ShapeDtypeStruct((WIN * STEP, 2 * NF), jnp.float32),
        in_specs=[in_vmem()] * 3,
        out_specs=in_vmem(),
        compiler_params=params(),
        cost_estimate=pl.CostEstimate(flops=0, bytes_accessed=1000, transcendentals=0),
    )(rows, even, odd)


def correlate_between(bit, rows, left, matching, even, odd, inverse):
    return pl.pallas_call(
        functools.partial(between_kernel, bit),
        out_shape=OUT,
        in_specs=[in_vmem()] * 6,
        out_specs=in_vmem(),
        scratch_shapes=[CROSS],
        compiler_params=params(),
        cost_estimate=pl.CostEstimate(flops=0, bytes_accessed=1000, transcendentals=0),
    )(rows, left, matching, even, odd, inverse)


def correlate_within(rows, left, even, odd, inverse, between):
    return pl.pallas_call(
        within_kernel,
        out_shape=[OUT, OUT],
        in_specs=[in_vmem()] * 6,
        out_specs=[in_vmem(), pl.BlockSpec(memory_space=pl.ANY)],
        scratch_shapes=[CROSS, pltpu.SemaphoreType.DMA],
        compiler_params=params(),
        cost_estimate=pl.CostEstimate(flops=0, bytes_accessed=1000, transcendentals=0),
    )(rows, left, even, odd, inverse, between)


def shards(groups, blocks, traces, assign, matching):
    even = jnp.asarray(forward_table(EVEN_BINS))
    odd = jnp.asarray(forward_table(ODD_BINS))
    inverse = jnp.asarray(inverse_table())
    long_rows, rows = order_rows(traces, assign)
    beside = lax.ppermute(long_rows, "blk", [((i - 1) % blocks, i) for i in range(blocks)])
    remote = rows
    bit = 1
    while True:
        other = lax.ppermute(remote, "group", [(g ^ bit, g) for g in range(groups)])
        if bit * 2 >= groups:
            break
        remote = jnp.where((matching[0, 0] & bit) != 0, other, remote)
        bit *= 2
    left = own_spectra(rows, even, odd)
    between = correlate_between(bit, other, left, matching, even, odd, inverse)
    within, between = correlate_within(beside, left, even, odd, inverse, between)
    return (between.transpose(0, 3, 1, 2, 4), within.transpose(0, 3, 1, 2, 4))


def solution(mesh):
    placed = (P(("group", "blk"), None, None, None), P(("group", "blk")), P("blk", None))
    return jax.shard_map(
        functools.partial(shards, mesh.shape["group"], mesh.shape["blk"]),
        mesh=mesh,
        in_specs=placed,
        out_specs=(
            P(("group", "blk"), None, None, None, None),
            P(("group", "blk"), None, None, None, None),
        ),
        check_vma=False,
    )
```

time: 17 us -> 11.1 us (0.65)
  the two profiles are of different devices: /device:TPU:1 before, /device:TPU:0 now
where the time goes in v2:
time: 11.1 us; the launch traced here: 11 us
  Pallas kernels  4.53 us (41%)
  starting transfers between devices  3.09 us (28%)
  waiting for transfers between devices  2.68 us (24%)
  between operations  0.67 us (6%)
    ppermute x1, starting transfers between devices, shards(): other = lax.ppermute(remote, 'group', [(g ^ bit, g) for g in range(groups)])  2.59 us
    pallas_call x1, Pallas kernels, correlate_within(): pl.pallas_call(within_kernel, out_shape=[OUT, OUT], in_specs=[in_vmem()]...  1.77 us
    ppermute x1, waiting for transfers between devices, shards(): other = lax.ppermute(remote, 'group', [(g ^ bit, g) for g in range(groups)])  1.63 us
    pallas_call x1, Pallas kernels, order_rows(): pl.pallas_call(order_kernel, out_shape=[jax.ShapeDtypeStruct((WIN * STEP,...  1.15 us
    ppermute x1, waiting for transfers between devices, shards(): lax.ppermute(long_rows, 'blk', [((i - 1) % blocks, i) for i in range(bloc...  1.06 us
    pallas_call x1, Pallas kernels, correlate_between(): pl.pallas_call(functools.partial(between_kernel, bit), out_shape=OUT, in_...  1.04 us
    pallas_call x1, Pallas kernels, own_spectra(): pl.pallas_call(own_kernel, out_shape=jax.ShapeDtypeStruct((WIN * STEP, 2...  0.57 us
    ppermute x1, starting transfers between devices, shards(): lax.ppermute(long_rows, 'blk', [((i - 1) % blocks, i) for i in range(bloc...  0.5 us
  transfers between devices with their start and end apart: 2, of which 2 were waited for; matrix products, arithmetic and copies ran while one was open for 0% of the time, Pallas kernels for 15%

profile of v2, /device:TPU:0, one launch (start us, length us, event | category | flops | bytes accessed | tf_op | source)
XLA Modules:
  0.0 11.0 jit_solution(9353461582164560381)
XLA Ops:
  0.6 0.0 copy-start
  0.6 0.0 copy-start.1
  0.7 1.2 %shard_map.77 = (bf16[24,1280]{1,0:T(8,128)(2,1)S(1)}, bf16[24,1200]{1,0:T(8,128)(2,1)S(1)}) custom-call(bf16[4,3,2,1200]{3,2,1,0:T(2,128)(2,1)} %traces_ref.1, s32[1,4]{1,0:T(1,128)} %bitcast.5), custom_call_target="tpu_custom_call" | custom-call | flops 8000000000 | bytes 20000000 | tf_op jit(solution)/shard_map/pallas_call | solution.py:157
  1.8 0.5 %collective-permute-start = (bf16[24,1280]{1,0:T(8,128)(2,1)S(1)}, bf16[24,1280]{1,0:T(8,128)(2,1)S(1)}, u32[]{:S(2)}, u32[]{:S(2)}) collective-permute-start(bf16[24,1280]{1,0:T(8,128)(2,1)S(1)} %get-tuple-element.6), channel_id=1, source_target_pairs={{15,0},{0,1},{1,2},{2,3},{3,4},{4,5},{5,6},{6,7},{7,8},{8,9},{9,10... | collective-permute-start | bytes 184328 | tf_op jit(solution)/shard_map/ppermute | solution.py:218
  2.3 0.0 copy-start.2
  2.3 0.0 copy-start.3
  2.3 2.6 %collective-permute-start.1 = (bf16[24,1200]{1,0:T(8,128)(2,1)S(1)}, bf16[24,1200]{1,0:T(8,128)(2,1)S(1)}, u32[]{:S(2)}, u32[]{:S(2)}) collective-permute-start(bf16[24,1200]{1,0:T(8,128)(2,1)S(1)} %get-tuple-element.7.rows_ref), channel_id=1, source_target_pairs={{16,0},{0,16},{17,1},{1,17},{18,2},{2,18},{19,3},{3,19},{20,4},{4,... | collective-permute-start | bytes 172808 | tf_op jit(solution)/shard_map/ppermute | solution.py:222
  4.9 0.0 copy-done
  4.9 0.0 copy-done.1
  4.9 0.6 %shard_map.78.left_ref = f32[24,1536]{1,0:T(8,128)S(1)} custom-call(bf16[24,1200]{1,0:T(8,128)(2,1)S(1)} %get-tuple-element.7.rows_ref, bf16[768,768]{1,0:T(8,128)(2,1)S(1)} %copy-done.1, bf16[768,768]{1,0:T(8,128)(2,1)S(1)} %copy-done), custom_call_target="tpu_custom_call" | custom-call | bytes 1000 | tf_op jit(solution)/shard_map/pallas_call | solution.py:179
  5.5 1.6 %collective-permute-done.1.rows_ref = bf16[24,1200]{1,0:T(8,128)(2,1)S(1)} collective-permute-done((bf16[24,1200]{1,0:T(8,128)(2,1)S(1)}, bf16[24,1200]{1,0:T(8,128)(2,1)S(1)}, u32[]{:S(2)}, u32[]{:S(2)}) %collective-permute-start.1) | collective-permute-done | bytes 57632 | tf_op jit(solution)/shard_map/ppermute | solution.py:222
  7.1 0.0 copy-done.2
  7.1 0.0 copy-done.3
  7.1 1.0 %shard_map.79.between_ref = bf16[4,3,3,4,401]{4,3,2,1,0:T(4,128)(2,1)S(1)} custom-call(bf16[24,1200]{1,0:T(8,128)(2,1)S(1)} %collective-permute-done.1.rows_ref, f32[24,1536]{1,0:T(8,128)S(1)} %shard_map.78.left_ref, s32[1,2]{1,0:T(1,128)S(1)} %copy-done.3, bf16[768,768]{1,0:T(8,128)(2,1)S(1)} %copy-done.1, bf16[768,768]{1,0:T(8,128)(2,1)S(1)} %copy-done, ...), custom_call_target="tpu_custom_call" | custom-call | bytes 1000 | tf_op jit(solution)/shard_map/pallas_call | solution.py:190
  8.2 1.1 %collective-permute-done.rows_ref = bf16[24,1280]{1,0:T(8,128)(2,1)S(1)} collective-permute-done((bf16[24,1280]{1,0:T(8,128)(2,1)S(1)}, bf16[24,1280]{1,0:T(8,128)(2,1)S(1)}, u32[]{:S(2)}, u32[]{:S(2)}) %collective-permute-start) | collective-permute-done | bytes 61472 | tf_op jit(solution)/shard_map/ppermute | solution.py:218
  9.2 1.8 %shard_map.80 = (bf16[4,3,3,4,401]{4,3,2,1,0:T(4,128)(2,1)}, bf16[4,3,3,4,401]{4,3,2,1,0:T(4,128)(2,1)}) custom-call(bf16[24,1280]{1,0:T(8,128)(2,1)S(1)} %collective-permute-done.rows_ref, f32[24,1536]{1,0:T(8,128)S(1)} %shard_map.78.left_ref, bf16[768,768]{1,0:T(8,128)(2,1)S(1)} %copy-done.1, bf16[768,768]{1,0:T(8,128)(2,1)S(1)} %copy-done, ...), custom_call_target="tpu_custom_call" | custom-call | bytes 1000 | tf_op jit(solution)/shard_map/pallas_call | solution.py:202
Async XLA Ops:
  0.6 4.3 %copy-start = (bf16[768,768]{1,0:T(8,128)(2,1)S(1)}, bf16[768,768]{1,0:T(8,128)(2,1)}, u32[]{:S(2)}) copy-start(bf16[768,768]{1,0:T(8,128)(2,1)} %constant.7.clone.odd_ref) | copy-start | bytes 3538948
  0.6 4.3 %copy-start.1 = (bf16[768,768]{1,0:T(8,128)(2,1)S(1)}, bf16[768,768]{1,0:T(8,128)(2,1)}, u32[]{:S(2)}) copy-start(bf16[768,768]{1,0:T(8,128)(2,1)} %constant.6.clone.even_ref) | copy-start | bytes 3538948
  1.8 7.4 %collective-permute-start = (bf16[24,1280]{1,0:T(8,128)(2,1)S(1)}, bf16[24,1280]{1,0:T(8,128)(2,1)S(1)}, u32[]{:S(2)}, u32[]{:S(2)}) collective-permute-start(bf16[24,1280]{1,0:T(8,128)(2,1)S(1)} %get-tuple-element.6), channel_id=1, source_target_pairs={{15,0},{0,1},{1,2},{2,3},{3,4},{4,5},{5,6},{6,7},{7,8},{8,9},{9,10... | collective-permute-start | bytes 184328 | tf_op jit(solution)/shard_map/ppermute | solution.py:218
  2.3 4.8 %copy-start.2 = (bf16[1536,401]{1,0:T(8,128)(2,1)S(1)}, bf16[1536,401]{1,0:T(8,128)(2,1)}, u32[]{:S(2)}) copy-start(bf16[1536,401]{1,0:T(8,128)(2,1)} %constant.8.clone.inverse_ref) | copy-start | bytes 3695620
  2.3 4.8 %copy-start.3 = (s32[1,2]{1,0:T(1,128)S(1)}, s32[1,2]{1,0:T(1,128)}, u32[]{:S(2)}) copy-start(s32[1,2]{1,0:T(1,128)} %matching_ref.1) | copy-start | bytes 28
  2.3 4.8 %collective-permute-start.1 = (bf16[24,1200]{1,0:T(8,128)(2,1)S(1)}, bf16[24,1200]{1,0:T(8,128)(2,1)S(1)}, u32[]{:S(2)}, u32[]{:S(2)}) collective-permute-start(bf16[24,1200]{1,0:T(8,128)(2,1)S(1)} %get-tuple-element.7.rows_ref), channel_id=1, source_target_pairs={{16,0},{0,16},{17,1},{1,17},{18,2},{2,18},{19,3},{3,19},{20,4},{4,... | collective-permute-start | bytes 172808 | tf_op jit(solution)/shard_map/ppermute | solution.py:222
